TPU v7x, 32 devices: a whole 2x2x4 slice. The times are simulated.
32 devices in a mesh: dp: 8 (over z, x), tensor: 4 (over y, core).
Axes of the slice: x: 2, y: 2, z: 4, core: 2. Of those that a mesh axis runs over, the one named last changes fastest.
Arguments:
- tokens: bfloat16 [2048, 1024], P('dp'), may hold values from -6 to 6
- cotangent: bfloat16 [2048, 1024], P('dp'), may hold values from -6 to 6
- seq_lengths: int32 [8, 3], P('dp'), may hold values from 1 to 224, 256 in all within a row
- routes: int32 [2048, 8], P('dp'), may hold values from 0 to 31, all different within a row; in each aligned block of 256 rows (0 to 255, 256 to 511, ...) at most 80 rows name the same one
- gates: float32 [2048, 8], P('dp'), may hold values from 0 to 1, as said below
- norm1_gain: float32 [1024], replicated, may hold values from 0.5 to 1.5
- w_query: bfloat16 [1024, 1024], P(None, 'tensor'), may hold values from -0.1875 to 0.1875
- key_weight: bfloat16 [1024, 512], P(None, 'tensor'), may hold values from -0.1875 to 0.1875
- value_weight: bfloat16 [1024, 512], P(None, 'tensor'), may hold values from -0.1875 to 0.1875
- w_output: bfloat16 [1024, 1024], P('tensor'), may hold values from -0.75 to 0.75
- norm2_gain: float32 [1024], replicated, may hold values from 0.5 to 1.5
- w_gate: bfloat16 [32, 1024, 512], P('dp', None, 'tensor'), may hold values from -0.1875 to 0.1875
- w_up: bfloat16 [32, 1024, 512], P('dp', None, 'tensor'), may hold values from -0.1875 to 0.1875
- w_down: bfloat16 [32, 512, 1024], P('dp', 'tensor'), may hold values from -1 to 1
Outputs:
- layer_out: bfloat16 [2048, 1024], P('dp')
- d_tokens: float32 [2048, 1024], P('dp')
- d_norm1_gain: float32 [1024], replicated
- d_w_query: float32 [1024, 1024], P(None, 'tensor')
- d_w_key: float32 [1024, 512], P(None, 'tensor')
- d_w_value: float32 [1024, 512], P(None, 'tensor')
- d_w_output: float32 [1024, 1024], P('tensor')
- d_norm2_gain: float32 [1024], replicated
- d_w_gate: float32 [32, 1024, 512], P('dp', None, 'tensor')
- d_w_up: float32 [32, 1024, 512], P('dp', None, 'tensor')
- d_w_down: float32 [32, 512, 1024], P('dp', 'tensor')
Inputs may be any that keep to these rules, and one draw needn't show every extreme that they name: `seq_lengths`: each index of dp has 3 sequences whose lengths sum to 256; on every index the longest is exactly 224. `routes`: each row names 8 different experts. Among the 256 rows of one index of dp no expert is named more than 80 times, and in every draw some index names some expert exactly 80 times. `gates`: each row is positive and sums to one.
All inputs are finite; a program needn't handle non-finite values.
Results may differ from a plain program's by a relative error of at most 0.015.
Values may be sent and summed in bfloat16 or wider, within the bound.
A program may use at most 192 MiB of HBM per device.

v0:
```python
import jax
import jax.numpy as jnp
from jax import lax
from jax.sharding import PartitionSpec as P

HEAD_SIZE = 64
EXPERTS = 32
TOPK = 8
SLOT = 80


EPSILON = 1e-05
ROPE_BASE = 10000.0


def layout(lengths, row_total):
    seq_ends = jnp.cumsum(lengths)
    seq_starts = seq_ends - lengths
    row_ids = jnp.arange(row_total, dtype=jnp.int32)
    segment = jnp.sum((row_ids[:, None] >= seq_ends[None, :]).astype(jnp.int32), axis=1)
    member = segment[:, None] == jnp.arange(lengths.shape[0], dtype=jnp.int32)[None, :]
    seq_begin = jnp.sum(jnp.where(member, seq_starts[None, :], 0), axis=1)
    position = row_ids - seq_begin
    allowed = (segment[:, None] == segment[None, :]) & (row_ids[None, :] <= row_ids[:, None])
    return (position, allowed)


def rotary(position, width):
    half_width = width // 2
    frequency = ROPE_BASE ** (-2.0 * jnp.arange(half_width, dtype=jnp.float32) / width)
    angles = position.astype(jnp.float32)[:, None] * frequency[None, :]
    return (jnp.cos(angles), jnp.sin(angles))


def apply_rotation(rows_three, cosine_table, sine_table):
    half_width = rows_three.shape[-1] // 2
    first_half = rows_three[..., :half_width]
    second_half = rows_three[..., half_width:]
    cos_rows = cosine_table[:, None, :]
    sin_rows = sine_table[:, None, :]
    return jnp.concatenate(
        [
            first_half * cos_rows - second_half * sin_rows,
            second_half * cos_rows + first_half * sin_rows,
        ],
        axis=-1,
    )


def norm_back(grad_out, unit_rows, inv_rms, gain_vec):
    scaled = grad_out * gain_vec
    return inv_rms * (scaled - unit_rows * jnp.mean(scaled * unit_rows, axis=-1, keepdims=True))


def swish_parts(gate_pre):
    sigmoid_gate = jax.nn.sigmoid(gate_pre)
    return (gate_pre * sigmoid_gate, sigmoid_gate * (1.0 + gate_pre * (1.0 - sigmoid_gate)))


def all_slots(slot_rows):
    return lax.all_gather(slot_rows, "tensor", axis=0, tiled=True)


def slot_sum(term_fn, depth):
    return lax.psum_scatter(
        term_fn(jnp.int32(0), lax.axis_size("tensor") * depth),
        "tensor",
        scatter_dimension=0,
        tiled=True,
    )


def body(
    tokens,
    cotangent,
    seq_lengths,
    routes,
    gates,
    norm1_gain,
    w_query,
    key_weight,
    value_weight,
    w_output,
    norm2_gain,
    w_gate,
    w_up,
    w_down,
):
    rows_count = tokens.shape[0]
    width = tokens.shape[1]
    query_heads = w_query.shape[1] // HEAD_SIZE
    kv_heads = key_weight.shape[1] // HEAD_SIZE
    head_group = query_heads // kv_heads
    local_experts = w_gate.shape[0]
    sources = lax.axis_size("dp")
    members = lax.axis_size("tensor")
    member_id = lax.axis_index("tensor")
    quarter = SLOT // members
    score_scale = HEAD_SIZE ** (-0.5)
    position, allowed = layout(seq_lengths.reshape(-1), rows_count)
    cosine_table, sine_table = rotary(position, HEAD_SIZE)
    inputs = tokens.astype(jnp.float32)
    inv_rms1 = lax.rsqrt(jnp.mean(inputs * inputs, axis=-1, keepdims=True) + EPSILON)
    unit1 = inputs * inv_rms1
    normalized_input = (unit1 * norm1_gain).astype(jnp.bfloat16)
    query_unrotated = jnp.dot(
        normalized_input, w_query, preferred_element_type=jnp.float32
    ).reshape(rows_count, query_heads, HEAD_SIZE)
    key_unrotated = jnp.dot(
        normalized_input, key_weight, preferred_element_type=jnp.float32
    ).reshape(rows_count, kv_heads, HEAD_SIZE)
    query_matrix = (
        apply_rotation(query_unrotated, cosine_table, sine_table)
        .astype(jnp.bfloat16)
        .reshape(rows_count, kv_heads, head_group, HEAD_SIZE)
    )
    key_rows = apply_rotation(key_unrotated, cosine_table, sine_table).astype(jnp.bfloat16)
    value_matrix = (
        jnp.dot(normalized_input, value_weight, preferred_element_type=jnp.float32)
        .astype(jnp.bfloat16)
        .reshape(rows_count, kv_heads, HEAD_SIZE)
    )

    def attention_scores():
        raw_scores = (
            jnp.einsum("qkgd,skd->kgqs", query_matrix, key_rows, preferred_element_type=jnp.float32)
            * score_scale
        )
        return jnp.where(allowed, raw_scores, -1000000000.0)

    scores = attention_scores()
    top_score = jnp.max(scores, axis=-1, keepdims=True)
    exponent = jnp.exp(scores - top_score)
    denominator = jnp.sum(exponent, axis=-1, keepdims=True)
    prob_low = (exponent / denominator).astype(jnp.bfloat16)
    log_total = top_score + jnp.log(denominator)
    mixed_heads = jnp.einsum(
        "kgqs,skd->qkgd", prob_low, value_matrix, preferred_element_type=jnp.float32
    )
    mixed_heads = mixed_heads.reshape(rows_count, query_heads * HEAD_SIZE).astype(jnp.bfloat16)
    attended = lax.psum(
        jnp.dot(mixed_heads, w_output, preferred_element_type=jnp.float32), "tensor"
    )
    hidden = inputs + attended
    inv_rms2 = lax.rsqrt(jnp.mean(hidden * hidden, axis=-1, keepdims=True) + EPSILON)
    unit2 = hidden * inv_rms2
    normed2 = (unit2 * norm2_gain).astype(jnp.bfloat16)
    flat_routes = routes.reshape(-1)
    onehot = (flat_routes[:, None] == jnp.arange(EXPERTS, dtype=jnp.int32)[None, :]).astype(
        jnp.int32
    )
    rank_in = jnp.sum((jnp.cumsum(onehot, axis=0) - onehot) * onehot, axis=1)
    mine = rank_in // quarter == member_id
    place = (rank_in - member_id * quarter) * EXPERTS + flat_routes
    target = jnp.where(mine, place, quarter * EXPERTS)
    lookup = jnp.where(mine, place, 0)
    route_token = jnp.arange(flat_routes.shape[0], dtype=jnp.int32) // TOPK
    source = jnp.zeros((quarter * EXPERTS,), jnp.int32).at[target].set(route_token, mode="drop")
    occupied = jnp.zeros((quarter * EXPERTS,), jnp.int32).at[target].set(1, mode="drop") > 0
    gate_slot = (
        jnp.zeros((quarter * EXPERTS,), jnp.float32).at[target].set(gates.reshape(-1), mode="drop")
    )
    gates_mine = jnp.where(mine, gates.reshape(-1), 0.0).reshape(rows_count, TOPK)
    outgoing = jnp.where(occupied[:, None], normed2[source], 0).reshape(quarter, EXPERTS, width)
    arrived = lax.all_to_all(outgoing, "dp", split_axis=1, concat_axis=1, tiled=True)
    grouped = all_slots(arrived).reshape(SLOT, sources, local_experts, width)
    gate_pre = jnp.einsum("sped,edf->spef", grouped, w_gate, preferred_element_type=jnp.float32)
    up_pre = jnp.einsum("sped,edf->spef", grouped, w_up, preferred_element_type=jnp.float32)
    activated = (jax.nn.silu(gate_pre) * up_pre).astype(jnp.bfloat16)

    def output_term(first_row, how_many):
        produced_part = jnp.einsum(
            "spef,efd->sped", activated, w_down, preferred_element_type=jnp.float32
        )
        return produced_part.reshape(how_many, sources * local_experts, width)

    produced = slot_sum(output_term, quarter).astype(jnp.bfloat16)
    returned = lax.all_to_all(produced, "dp", split_axis=1, concat_axis=1, tiled=True)
    routed = returned.reshape(quarter * EXPERTS, width)[lookup].reshape(rows_count, TOPK, width)
    partial_mix = jnp.sum(gates_mine[:, :, None] * routed.astype(jnp.float32), axis=1)
    mixture = lax.psum(partial_mix, "tensor")
    result = hidden + mixture
    upstream = cotangent.astype(jnp.float32)
    grad_outgoing = jnp.where(occupied[:, None], gate_slot[:, None] * upstream[source], 0.0)
    grad_outgoing = grad_outgoing.astype(jnp.bfloat16).reshape(quarter, EXPERTS, width)
    grad_arrived = lax.all_to_all(grad_outgoing, "dp", split_axis=1, concat_axis=1, tiled=True)
    grad_four = all_slots(grad_arrived).reshape(SLOT, sources, local_experts, width)
    grad_act = jnp.einsum("sped,efd->spef", grad_four, w_down, preferred_element_type=jnp.float32)
    swish, slope = swish_parts(gate_pre)
    grad_gate = (grad_act * up_pre * slope).astype(jnp.bfloat16)
    grad_up = (grad_act * swish).astype(jnp.bfloat16)

    def input_term(first_row, how_many):
        term = jnp.einsum("spef,edf->sped", grad_gate, w_gate, preferred_element_type=jnp.float32)
        term = term + jnp.einsum(
            "spef,edf->sped", grad_up, w_up, preferred_element_type=jnp.float32
        )
        return term.reshape(how_many, sources * local_experts, width)

    grad_rows = slot_sum(input_term, quarter).astype(jnp.bfloat16)
    d_gate = jnp.einsum("sped,spef->edf", grouped, grad_gate, preferred_element_type=jnp.float32)
    d_up = jnp.einsum("sped,spef->edf", grouped, grad_up, preferred_element_type=jnp.float32)
    d_down = jnp.einsum("spef,sped->efd", activated, grad_four, preferred_element_type=jnp.float32)
    grad_home = lax.all_to_all(grad_rows, "dp", split_axis=1, concat_axis=1, tiled=True)
    routed_grad = grad_home.reshape(quarter * EXPERTS, width)[lookup].reshape(
        rows_count, TOPK, width
    )
    mine_rows = mine.reshape(rows_count, TOPK)[:, :, None]
    partial_grad = jnp.sum(jnp.where(mine_rows, routed_grad.astype(jnp.float32), 0.0), axis=1)
    grad_norm2 = lax.psum(partial_grad, "tensor")
    grad_hidden = upstream + norm_back(grad_norm2, unit2, inv_rms2, norm2_gain)
    d_norm2 = jnp.sum(grad_norm2 * unit2, axis=0)
    grad_attended = grad_hidden.astype(jnp.bfloat16)
    d_output = jnp.einsum(
        "rh,rd->hd", mixed_heads, grad_attended, preferred_element_type=jnp.float32
    )
    grad_mixed = jnp.einsum(
        "rd,hd->rh", grad_attended, w_output, preferred_element_type=jnp.float32
    )
    grad_mixed = grad_mixed.astype(jnp.bfloat16).reshape(
        rows_count, kv_heads, head_group, HEAD_SIZE
    )
    prob_full = jnp.where(allowed, jnp.exp(attention_scores() - log_total), 0.0)
    prob_again = prob_full.astype(jnp.bfloat16)
    grad_probs = jnp.einsum(
        "qkgd,skd->kgqs", grad_mixed, value_matrix, preferred_element_type=jnp.float32
    )
    grad_values = jnp.einsum(
        "kgqs,qkgd->skd", prob_again, grad_mixed, preferred_element_type=jnp.float32
    )
    grad_values = grad_values.astype(jnp.bfloat16).reshape(rows_count, kv_heads * HEAD_SIZE)
    inner_sum = jnp.sum(grad_probs * prob_full, axis=-1, keepdims=True)
    grad_scores = (prob_full * (grad_probs - inner_sum)).astype(jnp.bfloat16)
    grad_queries = (
        jnp.einsum("kgqs,skd->qkgd", grad_scores, key_rows, preferred_element_type=jnp.float32)
        * score_scale
    )
    grad_keys = (
        jnp.einsum("kgqs,qkgd->skd", grad_scores, query_matrix, preferred_element_type=jnp.float32)
        * score_scale
    )
    grad_qpre = apply_rotation(
        grad_queries.reshape(rows_count, query_heads, HEAD_SIZE), cosine_table, -sine_table
    )
    grad_qpre = grad_qpre.astype(jnp.bfloat16).reshape(rows_count, query_heads * HEAD_SIZE)
    grad_kpre = (
        apply_rotation(grad_keys, cosine_table, -sine_table)
        .astype(jnp.bfloat16)
        .reshape(rows_count, kv_heads * HEAD_SIZE)
    )
    d_query = jnp.einsum(
        "rd,rf->df", normalized_input, grad_qpre, preferred_element_type=jnp.float32
    )
    d_key = jnp.einsum("rd,rf->df", normalized_input, grad_kpre, preferred_element_type=jnp.float32)
    d_value = jnp.einsum(
        "rd,rf->df", normalized_input, grad_values, preferred_element_type=jnp.float32
    )
    grad_normed = jnp.einsum("rf,df->rd", grad_qpre, w_query, preferred_element_type=jnp.float32)
    grad_normed = grad_normed + jnp.einsum(
        "rf,df->rd", grad_kpre, key_weight, preferred_element_type=jnp.float32
    )
    grad_normed = grad_normed + jnp.einsum(
        "rf,df->rd", grad_values, value_weight, preferred_element_type=jnp.float32
    )
    grad_norm1 = lax.psum(grad_normed, "tensor")
    grad_tokens = grad_hidden + norm_back(grad_norm1, unit1, inv_rms1, norm1_gain)
    d_norm1 = jnp.sum(grad_norm1 * unit1, axis=0)
    summed = lax.psum((d_query, d_key, d_value, d_output, d_norm1, d_norm2), "dp")
    return (
        result.astype(jnp.bfloat16),
        grad_tokens,
        summed[4],
        summed[0],
        summed[1],
        summed[2],
        summed[3],
        summed[5],
        d_gate,
        d_up,
        d_down,
    )


def solution(mesh):
    in_specs = (
        P("dp", None),
        P("dp", None),
        P("dp", None),
        P("dp", None),
        P("dp", None),
        P(),
        P(None, "tensor"),
        P(None, "tensor"),
        P(None, "tensor"),
        P("tensor", None),
        P(),
        P("dp", None, "tensor"),
        P("dp", None, "tensor"),
        P("dp", "tensor", None),
    )
    out_specs = (
        P("dp", None),
        P("dp", None),
        P(),
        P(None, "tensor"),
        P(None, "tensor"),
        P(None, "tensor"),
        P("tensor", None),
        P(),
        P("dp", None, "tensor"),
        P("dp", None, "tensor"),
        P("dp", "tensor", None),
    )
    return jax.shard_map(body, mesh=mesh, in_specs=in_specs, out_specs=out_specs, check_vma=False)
```

profile of v0, /device:TPU:0, one launch (start us, length us, event | category | flops | bytes accessed | tf_op | source)
XLA Modules:
  0.0 679.4 jit_solution(3855707910559953157)
XLA Ops:
  9.5 9.1 %reduce-window.11 = s32[32,16,128]{2,1,0:T(8,128)S(1)} reduce-window(s32[32,16,128]{2,1,0:T(8,128)S(1)} %fusion.67, s32[]{:T(128)} %constant.61.clone.1), window={size=1x1x128 pad=0_0x0_0x127_0}, to_apply=%region_7.8 | reduce-window | flops 8323072 | bytes 524292 | tf_op jit(solution)/shard_map/reduce-window.1
  20.1 8.0 %scatter_custom_fusion.1 = s32[640]{0:T(1024)S(1)} fusion(s32[2048]{0:T(1024)S(1)} %bitcast.204, s32[2048]{0:T(1024)S(1)} %add_select_fusion.1, s32[]{:T(128)} %constant.61.clone.1), kind=kCustom, calls=%fused_computation.151 | custom fusion | bytes 2564 | tf_op jit(solution)/shard_map/scatter | solution.py:158
  28.1 8.0 %scatter_custom_fusion = s32[640]{0:T(1024)S(1)} fusion(s32[2048]{0:T(1024)S(1)} %bitcast.205, s32[2048]{0:T(1024)S(1)} %ne.62, s32[]{:T(128)} %constant.61.clone.1), kind=kCustom, calls=%fused_computation.154 | custom fusion | bytes 2564 | tf_op jit(solution)/shard_map/scatter | solution.py:159
  36.4 8.0 %scatter_custom_fusion.2 = f32[640]{0:T(1024)S(1)} fusion(s32[2048]{0:T(1024)S(1)} %bitcast.206, f32[2048]{0:T(1024)S(1)} %reshape.450, f32[]{:T(128)} %constant.30.clone.1), kind=kCustom, calls=%fused_computation.149 | custom fusion | bytes 2564 | tf_op jit(solution)/shard_map/scatter | solution.py:161
  44.7 3.5 gather_fusion.2
  48.2 4.5 fusion.11
  52.7 7.4 %all-to-all-start.2 = ((bf16[20,32,1024]{2,0,1:T(8,128)(2,1)}), bf16[20,32,1024]{2,0,1:T(8,128)(2,1)}, u32[]{:S(2)}, u32[]{:S(2)}) async-start(bf16[20,32,1024]{2,0,1:T(8,128)(2,1)} %fusion.11), calls=%async_computation.3 | async-start | bytes 3145728 | tf_op jit(solution)/shard_map/all_to_all | solution.py:186
  65.3 32.0 %all-to-all-done.2 = bf16[20,32,1024]{2,0,1:T(8,128)(2,1)} async-done(((bf16[20,32,1024]{2,0,1:T(8,128)(2,1)}), bf16[20,32,1024]{2,0,1:T(8,128)(2,1)}, u32[]{:S(2)}, u32[]{:S(2)}) %all-to-all-start.2) | async-done | bytes 1310752 | tf_op jit(solution)/shard_map/all_to_all | solution.py:186
  105.1 3.5 gather_fusion
  111.0 41.7 %all_to_all.20 = bf16[20,32,1024]{2,0,1:T(8,128)(2,1)S(1)} all-to-all(bf16[20,32,1024]{2,0,1:T(8,128)(2,1)S(1)} %copy_select_fusion), channel_id=1, replica_groups=mesh['dp'=8,'tensor'=4] {'dp'}, dimensions={1} | all-to-all | bytes 2621440 | tf_op jit(solution)/shard_map/all_to_all | solution.py:165
  154.6 7.9 %copy.176 = bf16[80,32,1024]{2,0,1:T(8,128)(2,1)} copy(bf16[80,32,1024]{2,1,0:T(8,128)(2,1)} %all-gather.5.cloned.1.call-done) | data formatting | bytes 10485760 | tf_op jit(solution)/shard_map/all_gather | solution.py:61
  162.5 31.3 %all-gather.3.cloned.1.call-done = bf16[80,32,1024]{2,1,0:T(8,128)(2,1)} async-done(((bf16[20,32,1024]{2,1,0:T(8,128)(2,1)}), bf16[80,32,1024]{2,1,0:T(8,128)(2,1)}) %all-gather.3.cloned.1.call-update) | async-done | bytes 5242896 | tf_op jit(solution)/shard_map/all_gather | solution.py:61
  193.8 5.4 copy.164
  209.5 9.9 %copy.180 = f32[80,8,4,1024]{3,0,2,1:T(8,128)} copy(f32[80,8,4,1024]{3,1,0,2:T(8,128)S(1)} %add_bitcast_fusion) | data formatting | bytes 20971520 | tf_op jit(solution)/shard_map/add | solution.py:195
  219.5 14.3 %copy.181 = f32[80,32,1024]{2,1,0:T(8,128)} copy(f32[80,32,1024]{2,0,1:T(8,128)} %bitcast.165) | data formatting | bytes 20971520 | tf_op jit(solution)/shard_map/reshape | solution.py:198
  233.8 5.5 convolution_bitcast_fusion
  239.3 12.0 %copy.168 = f32[80,8,4,1024]{3,0,2,1:T(8,128)S(1)} copy(f32[80,8,4,1024]{3,1,0,2:T(8,128)} %convolution_bitcast_fusion) | data formatting | bytes 20971520 | tf_op jit(solution)/shard_map/spef,efd->sped/transpose | solution.py:172
  251.3 10.8 %copy.169 = f32[80,32,1024]{2,1,0:T(8,128)} copy(f32[80,32,1024]{2,0,1:T(8,128)S(1)} %bitcast.166) | data formatting | bytes 20971520 | tf_op jit(solution)/shard_map/reshape | solution.py:175
  262.2 57.0 %reduce-scatter.5.cloned.1.call-done = f32[20,32,1024]{2,1,0:T(8,128)} async-done(((f32[80,32,1024]{2,1,0:T(8,128)}), f32[20,32,1024]{2,1,0:T(8,128)}) %reduce-scatter.5.cloned.1.call-update) | async-done | bytes 2621456 | tf_op jit(solution)/shard_map/reduce_scatter | solution.py:65
  323.0 5.5 all-to-all-start.3
  328.5 78.6 %reduce-scatter.3.cloned.1.call-done = f32[20,32,1024]{2,1,0:T(8,128)} async-done(((f32[80,32,1024]{2,1,0:T(8,128)}), f32[20,32,1024]{2,1,0:T(8,128)}) %reduce-scatter.3.cloned.1.call-update) | async-done | bytes 2621456 | tf_op jit(solution)/shard_map/reduce_scatter | solution.py:65
  411.0 5.5 all-to-all-start.1
  419.0 9.6 %gather_fusion.3 = bf16[2048,1024]{1,0:T(8,128)(2,1)} fusion(bf16[640,1024]{1,0:T(8,128)(2,1)S(1)} %bitcast.164, s32[2048]{0:T(1024)S(1)} %broadcast_clamp_fusion), kind=kCustom, calls=%fused_computation.3 | custom fusion | bytes 8396800 | tf_op jit(solution)/shard_map/gather | solution.py:205
  428.6 5.3 fusion
  434.2 19.4 %all-to-all-done.1 = bf16[20,32,1024]{2,0,1:T(8,128)(2,1)} async-done(((bf16[20,32,1024]{2,0,1:T(8,128)(2,1)}), bf16[20,32,1024]{2,0,1:T(8,128)(2,1)}, u32[]{:S(2)}, u32[]{:S(2)}) %all-to-all-start.1) | async-done | bytes 1310752 | tf_op jit(solution)/shard_map/all_to_all | solution.py:178
  455.8 9.6 %gather_fusion.1 = bf16[2048,1024]{1,0:T(8,128)(2,1)} fusion(bf16[640,1024]{1,0:T(8,128)(2,1)S(1)} %bitcast.163, s32[2048]{0:T(1024)S(1)} %broadcast_clamp_fusion), kind=kCustom, calls=%fused_computation.1 | custom fusion | bytes 8396800 | tf_op jit(solution)/shard_map/gather | solution.py:179
  465.4 5.8 fusion.1
  484.9 5.2 fusion.12
  490.1 5.8 convolution_bitcast_fusion.1
  499.2 31.6 %all-reduce.14.cloned.1.call-done = (f32[256,1024]{1,0:T(8,128)}, f32[256,1024]{1,0:T(8,128)}) async-done(((f32[256,1024]{1,0:T(8,128)}, f32[256,1024]{1,0:T(8,128)}), (f32[256,1024]{1,0:T(8,128)}, f32[256,1024]{1,0:T(8,128)})) %all-reduce.14.cloned.1.call-update) | async-done | bytes 2097168 | tf_op jit(solution)/shard_map/psum | solution.py:181
  532.4 22.7 %all-reduce = (f32[1024]{0:T(1024)}, f32[1024]{0:T(1024)}) all-reduce(f32[1024]{0:T(1024)S(1)} %get-tuple-element.13, f32[1024]{0:T(1024)S(1)} %copy-done.55), channel_id=1, replica_groups=mesh['dp'=8,'tensor'=4] {'dp'}, use_global_device_ids=true, to_apply=%region_25.26 | all-reduce | flops 2048 | bytes 16384 | tf_op jit(solution)/shard_map/psum | solution.py:268
  558.1 108.1 %all-reduce.12.cloned.1.call-done = (f32[1024,256]{1,0:T(8,128)}, f32[1024,128]{1,0:T(8,128)}, f32[1024,128]{1,0:T(8,128)}, f32[256,1024]{1,0:T(8,128)}) async-done(((f32[1024,256]{1,0:T(8,128)}, f32[1024,128]{1,0:T(8,128)}, f32[1024,128]{1,0:T(8,128)}, f32[256,1024]{1,0:T(8,128)}), (f32[1024,256]{1,0:T(8,128)}, f32[1024,128]{1,0:T(8,128)}, f32[1024,128]{1,0:T(8,128)}, ...) | async-done | bytes 3145744 | tf_op jit(solution)/shard_map/psum | solution.py:268
  (242 shorter events, 71.1 us)
Async XLA Ops:
  7.2 196.2 %copy-start = (bf16[4,128,1024]{2,1,0:T(8,128)(2,1)S(1)}, bf16[4,128,1024]{2,1,0:T(8,128)(2,1)}, u32[]{:S(2)}) copy-start(bf16[4,128,1024]{2,1,0:T(8,128)(2,1)} %param.27) | copy-start | bytes 3145732
  7.2 37.4 %copy-start.11 = (bf16[256,1024]{1,0:T(8,128)(2,1)S(1)}, bf16[256,1024]{1,0:T(8,128)(2,1)}, u32[]{:S(2)}) copy-start(bf16[256,1024]{1,0:T(8,128)(2,1)} %param.15) | copy-start | bytes 1572868
  19.4 28.8 %copy-start.49 = (pred[2048]{0:T(1024)(128)(4,1)}, pred[2048]{0:T(1024)(128)(4,1)S(1)}, u32[]{:S(2)}) copy-start(pred[2048]{0:T(1024)(128)(4,1)S(1)} %fusion.72) | copy-start | bytes 6148
  36.2 12.0 %copy-start.44 = (s32[1024]{0:T(1024)}, s32[1024]{0:T(1024)S(1)}, u32[]{:S(2)}) copy-start(s32[1024]{0:T(1024)S(1)} %pad_clamp_fusion) | copy-start | bytes 12292
  36.4 11.8 %copy-start.42 = (pred[20,32]{0,1:T(8,128)(4,1)}, pred[20,32]{0,1:T(8,128)(4,1)S(1)}, u32[]{:S(2)}) copy-start(pred[20,32]{0,1:T(8,128)(4,1)S(1)} %copy.161) | copy-start | bytes 1924
  52.7 7.5 %copy-start.58 = (s32[1,3]{1,0:T(1,128)S(1)}, s32[1,3]{1,0:T(1,128)}, u32[]{:S(2)}) copy-start(s32[1,3]{1,0:T(1,128)} %param.16) | copy-start | bytes 40
  52.7 7.9 %copy-start.2 = (bf16[256,1024]{1,0:T(8,128)(2,1)S(1)}, bf16[256,1024]{1,0:T(8,128)(2,1)}, u32[]{:S(2)}) copy-start(bf16[256,1024]{1,0:T(8,128)(2,1)} %param.14) | copy-start | bytes 1572868
  52.7 8.3 %copy-start.29 = (bf16[1024,128]{1,0:T(8,128)(2,1)S(1)}, bf16[1024,128]{1,0:T(8,128)(2,1)}, u32[]{:S(2)}) copy-start(bf16[1024,128]{1,0:T(8,128)(2,1)} %param.21) | copy-start | bytes 786436
  52.7 8.3 %copy-start.39 = (f32[1024]{0:T(1024)S(1)}, f32[1024]{0:T(1024)}, u32[]{:S(2)}) copy-start(f32[1024]{0:T(1024)} %param.19) | copy-start | bytes 12292
  52.7 8.8 %copy-start.23 = (bf16[1024,256]{1,0:T(8,128)(2,1)S(1)}, bf16[1024,256]{1,0:T(8,128)(2,1)}, u32[]{:S(2)}) copy-start(bf16[1024,256]{1,0:T(8,128)(2,1)} %param.20) | copy-start | bytes 1572868
  52.7 44.5 %all-to-all-start.2 = ((bf16[20,32,1024]{2,0,1:T(8,128)(2,1)}), bf16[20,32,1024]{2,0,1:T(8,128)(2,1)}, u32[]{:S(2)}, u32[]{:S(2)}) async-start(bf16[20,32,1024]{2,0,1:T(8,128)(2,1)} %fusion.11), calls=%async_computation.3 | async-start | bytes 3145728 | tf_op jit(solution)/shard_map/all_to_all | solution.py:186
  60.1 42.7 %all-reduce.8.cloned.1.call-start = ((), (), s32[]{:S(2)}) async-start(), calls=%async_computation.6 | async-start | bytes 2097152 | tf_op jit(solution)/shard_map/psum | solution.py:141
  63.5 37.0 %copy-start.21 = (bf16[2,64,2,256]{3,1,2,0:T(8,128)(2,1)}, bf16[2,64,2,256]{3,1,2,0:T(8,128)(2,1)S(1)}, u32[]{:S(2)}) copy-start(bf16[2,64,2,256]{3,1,2,0:T(8,128)(2,1)S(1)} %convolution_convert_fusion.1) | copy-start | bytes 393220
  65.2 89.3 %all-gather.5.cloned.1.call-start = ((), (), s32[]{:S(2)}) async-start(), calls=%async_computation.9 | async-start | bytes 6553600 | tf_op jit(solution)/shard_map/all_gather | solution.py:61
  100.5 93.3 %all-gather.3.cloned.1.call-start = ((), (), s32[]{:S(2)}) async-start(), calls=%async_computation.7 | async-start | bytes 6553600 | tf_op jit(solution)/shard_map/all_gather | solution.py:61
  154.5 164.7 %reduce-scatter.5.cloned.1.call-start = ((), (), s32[]{:S(2)}) async-start(), calls=%async_computation.10 | async-start | bytes 13107200 | tf_op jit(solution)/shard_map/reduce_scatter | solution.py:65
  162.5 36.7 %copy-start.9 = (bf16[4,1024,128]{2,1,0:T(8,128)(2,1)S(1)}, bf16[4,1024,128]{2,1,0:T(8,128)(2,1)}, u32[]{:S(2)}) copy-start(bf16[4,1024,128]{2,1,0:T(8,128)(2,1)} %param.26) | copy-start | bytes 3145732
  206.1 27.8 %copy-start.8 = (bf16[80,8,4,128]{3,0,1,2:T(8,128)(2,1)}, bf16[80,8,4,128]{3,0,1,2:T(8,128)(2,1)S(1)}, u32[]{:S(2)}) copy-start(bf16[80,8,4,128]{3,0,1,2:T(8,128)(2,1)S(1)} %get-tuple-element.29) | copy-start | bytes 1966084
  233.8 173.4 %reduce-scatter.3.cloned.1.call-start = ((), (), s32[]{:S(2)}) async-start(), calls=%async_computation.8 | async-start | bytes 13107200 | tf_op jit(solution)/shard_map/reduce_scatter | solution.py:65
  323.0 88.0 %all-to-all-start.3 = ((bf16[20,32,1024]{2,0,1:T(8,128)(2,1)}), bf16[20,32,1024]{2,0,1:T(8,128)(2,1)}, u32[]{:S(2)}, u32[]{:S(2)}) async-start(bf16[20,32,1024]{2,0,1:T(8,128)(2,1)} %copy.182), calls=%async_computation.5 | async-start | bytes 3145728 | tf_op jit(solution)/shard_map/all_to_all | solution.py:204
  409.1 7.5 %copy-start.50 = (pred[2048]{0:T(1024)(128)(4,1)S(1)}, pred[2048]{0:T(1024)(128)(4,1)}, u32[]{:S(2)}) copy-start(pred[2048]{0:T(1024)(128)(4,1)} %copy-done.49) | copy-start | bytes 6148
  409.1 7.7 %copy-start.48 = (s32[2048,1]{0,1:T(1,128)S(1)}, s32[2048,1]{0,1:T(1,128)}, u32[]{:S(2)}) copy-start(s32[2048,1]{0,1:T(1,128)} %get-tuple-element.38) | copy-start | bytes 24580
  411.0 42.6 %all-to-all-start.1 = ((bf16[20,32,1024]{2,0,1:T(8,128)(2,1)}), bf16[20,32,1024]{2,0,1:T(8,128)(2,1)}, u32[]{:S(2)}, u32[]{:S(2)}) async-start(bf16[20,32,1024]{2,0,1:T(8,128)(2,1)} %copy.170), calls=%async_computation.2 | async-start | bytes 3145728 | tf_op jit(solution)/shard_map/all_to_all | solution.py:178
  416.5 54.7 %all-reduce.10.cloned.1.call-start = ((), (), s32[]{:S(2)}) async-start(), calls=%async_computation.11 | async-start | bytes 2097152 | tf_op jit(solution)/shard_map/psum | solution.py:210
  433.9 96.8 %all-reduce.14.cloned.1.call-start = ((), (), s32[]{:S(2)}) async-start(), calls=%async_computation.13 | async-start | bytes 4194304 | tf_op jit(solution)/shard_map/psum | solution.py:181
  465.4 5.8 copy-start.57
  479.3 187.0 %all-reduce.12.cloned.1.call-start = ((), (), s32[]{:S(2)}) async-start(), calls=%async_computation.12 | async-start | bytes 6291456 | tf_op jit(solution)/shard_map/psum | solution.py:268
  484.9 11.1 %slice-start.2 = ((s8[5242880]{0:T(1024)(128)(4,1)}), s8[4194304]{0:T(1024)(128)(4,1)S(1)}, s32[]{:S(2)}) async-start(s8[5242880]{0:T(1024)(128)(4,1)} %bitcast.175), calls=%async_computation.16 | async-start | bytes 8388608
  490.1 5.8 slice-start.3
  490.1 5.8 copy-start.19
  495.9 36.5 %copy-start.55 = (f32[1024]{0:T(1024)S(1)}, f32[1024]{0:T(1024)}, u32[]{:S(2)}) copy-start(f32[1024]{0:T(1024)} %get-tuple-element.11) | copy-start | bytes 12292
  666.3 6.1 copy-start.1
  (42 other events, 102.2 us)
Sparse Core Ops, SparseCore 0:
  65.3 37.4 all-reduce.7
  105.1 40.6 all-gather.4
  154.6 39.1 all-gather.2
  233.9 85.2 reduce-scatter.4
  321.8 85.2 reduce-scatter.2
  434.1 36.4 all-reduce.9
  479.4 51.2 all-reduce.13
  535.7 130.5 all-reduce.11
where the time goes:
time: 692 us; the launch traced here: 679 us
  waiting for transfers between devices  360 us (52%)
  local copies, waits for them, and re-layouts  136 us (20%)
  blocking collectives  64.5 us (9%)
  other arithmetic  43.7 us (6%)
  matrix products  40 us (6%)
  starting transfers between devices  19.6 us (3%)
  between operations  15.4 us (2%)
    reduce_scatter x2, waiting for transfers between devices, slot_sum(): lax.psum_scatter(term_fn(jnp.int32(0), lax.axis_size('tensor') * depth),...  136 us
    psum x1, waiting for transfers between devices, body(): lax.psum((d_query, d_key, d_value, d_output, d_norm1, d_norm2), 'dp')  108 us
    all_to_all x1, blocking collectives, body(): lax.all_to_all(outgoing, 'dp', split_axis=1, concat_axis=1, tiled=True)  41.7 us
    all_to_all x1, waiting for transfers between devices, body(): lax.all_to_all(grad_outgoing, 'dp', split_axis=1, concat_axis=1, tiled=True)  32 us
    psum x1, waiting for transfers between devices, body(): mixture = lax.psum(partial_mix, 'tensor')  31.6 us
    all_gather x2, waiting for transfers between devices, all_slots(): return lax.all_gather(slot_rows, 'tensor', axis=0, tiled=True)  31.4 us
    psum x1, blocking collectives, body(): lax.psum((d_query, d_key, d_value, d_output, d_norm1, d_norm2), 'dp')  22.7 us
    all_to_all x1, waiting for transfers between devices, body(): lax.all_to_all(produced, 'dp', split_axis=1, concat_axis=1, tiled=True)  19.4 us
  transfers between devices with their start and end apart: 11, of which 8 were waited for; matrix products, arithmetic and copies ran while one was open for 18% of the time, Pallas kernels for 0%

commit v1 on v0

v1 whole, which is shorter than its diff:
```python
import jax
import jax.numpy as jnp
from jax import lax
from jax.experimental import pallas as pl
from jax.experimental.pallas import tpu as pltpu
from jax.sharding import PartitionSpec as P

HEAD_SIZE = 64
EXPERTS = 32
LANES = 128
TILE = 512


EPSILON = 1e-05
ROPE_BASE = 10000.0


def layout(lengths, row_total):
    order = jnp.arange(lengths.shape[0], dtype=jnp.int32)
    seq_ends = jnp.sum(jnp.where(order[None, :] <= order[:, None], lengths[None, :], 0), axis=1)
    seq_starts = seq_ends - lengths
    row_ids = jnp.arange(row_total, dtype=jnp.int32)
    segment = jnp.sum((row_ids[:, None] >= seq_ends[None, :]).astype(jnp.int32), axis=1)
    member = segment[:, None] == jnp.arange(lengths.shape[0], dtype=jnp.int32)[None, :]
    seq_begin = jnp.sum(jnp.where(member, seq_starts[None, :], 0), axis=1)
    position = row_ids - seq_begin
    allowed = (segment[:, None] == segment[None, :]) & (row_ids[None, :] <= row_ids[:, None])
    return (position, allowed)


def rotary(position, width):
    half_width = width // 2
    frequency = ROPE_BASE ** (-2.0 * jnp.arange(half_width, dtype=jnp.float32) / width)
    angles = position.astype(jnp.float32)[:, None] * frequency[None, :]
    return (jnp.cos(angles), jnp.sin(angles))


def apply_rotation(rows_three, cosine_table, sine_table):
    half_width = rows_three.shape[-1] // 2
    first_half = rows_three[..., :half_width]
    second_half = rows_three[..., half_width:]
    cos_rows = cosine_table[:, None, :]
    sin_rows = sine_table[:, None, :]
    return jnp.concatenate(
        [
            first_half * cos_rows - second_half * sin_rows,
            second_half * cos_rows + first_half * sin_rows,
        ],
        axis=-1,
    )


def norm_back(grad_out, unit_rows, inv_rms, gain_vec):
    scaled = grad_out * gain_vec
    return inv_rms * (scaled - unit_rows * jnp.mean(scaled * unit_rows, axis=-1, keepdims=True))


def dot(left, right, left_dim, right_dim):
    return lax.dot_general(
        left,
        right,
        (((left_dim,), (right_dim,)), ((), ())),
        preferred_element_type=jnp.float32,
    )


def expert_kernel(
    rows_ref,
    cot_ref,
    gate_ref,
    pick_ref,
    w_gate_ref,
    w_up_ref,
    w_down_ref,
    mix_ref,
    grad_ref,
    d_gate_ref,
    d_up_ref,
    d_down_ref,
    weights,
    total,
):
    step = pl.program_id(0)
    experts, _, hidden_units = w_gate_ref.shape
    units = experts * hidden_units

    @pl.when(step == 0)
    def _():
        for e in range(experts):
            weights[:, e * hidden_units : (e + 1) * hidden_units] = w_gate_ref[e]
            weights[:, units + e * hidden_units : units + (e + 1) * hidden_units] = w_up_ref[e]
        total[...] = jnp.zeros_like(total)
        d_down_ref[...] = jnp.zeros_like(d_down_ref)

    rows = rows_ref[...]
    cot = cot_ref[...]
    gate = dot(gate_ref[...], pick_ref[...], 1, 0)
    gate_pre = dot(rows, weights[:, :units], 1, 0)
    up_pre = dot(rows, weights[:, units:], 1, 0)
    sigmoid_gate = jax.nn.sigmoid(gate_pre)
    swish = gate_pre * sigmoid_gate
    slope = sigmoid_gate * (1.0 + gate_pre * (1.0 - sigmoid_gate))
    activated = (swish * up_pre * gate).astype(jnp.bfloat16)
    grad_act = dot(cot, w_down_ref[...], 1, 1) * gate
    grad_gate = (grad_act * up_pre * slope).astype(jnp.bfloat16)
    grad_up = (grad_act * swish).astype(jnp.bfloat16)
    grad_rows = dot(grad_gate, weights[:, :units], 1, 1) + dot(grad_up, weights[:, units:], 1, 1)
    grad_ref[...] = grad_rows.astype(jnp.bfloat16)
    mix_ref[...] = dot(activated, w_down_ref[...], 1, 0).astype(jnp.bfloat16)
    total[:, :units] += dot(rows, grad_gate, 0, 0)
    total[:, units:] += dot(rows, grad_up, 0, 0)
    d_down_ref[...] += dot(activated, cot, 0, 0)

    @pl.when(step == pl.num_programs(0) - 1)
    def _():
        for e in range(experts):
            d_gate_ref[e] = total[:, e * hidden_units : (e + 1) * hidden_units]
            d_up_ref[e] = total[:, units + e * hidden_units : units + (e + 1) * hidden_units]


def experts_both_ways(rows, cot_gates, pick, w_gate, w_up, w_down):
    row_total, width = rows.shape
    experts, _, hidden_units = w_gate.shape
    units = experts * hidden_units
    tile = min(TILE, row_total)
    tiled = pl.BlockSpec((tile, width), lambda i: (i, 0))
    flat = pl.BlockSpec((units, width), lambda i: (0, 0))
    deep = pl.BlockSpec((experts, width, hidden_units), lambda i: (0, 0, 0))
    return pl.pallas_call(
        expert_kernel,
        grid=(row_total // tile,),
        in_specs=[
            tiled,
            tiled,
            pl.BlockSpec((tile, LANES), lambda i: (i, width // LANES)),
            pl.BlockSpec((LANES, units), lambda i: (0, 0)),
            deep,
            deep,
            flat,
        ],
        out_specs=[tiled, tiled, deep, deep, flat],
        out_shape=[
            jax.ShapeDtypeStruct((row_total, width), jnp.bfloat16),
            jax.ShapeDtypeStruct((row_total, width), jnp.bfloat16),
            jax.ShapeDtypeStruct(w_gate.shape, jnp.float32),
            jax.ShapeDtypeStruct(w_up.shape, jnp.float32),
            jax.ShapeDtypeStruct((units, width), jnp.float32),
        ],
        scratch_shapes=[
            pltpu.VMEM((width, 2 * units), jnp.bfloat16),
            pltpu.VMEM((width, 2 * units), jnp.float32),
        ],
        compiler_params=pltpu.CompilerParams(vmem_limit_bytes=56 * 2**20),
        cost_estimate=pl.CostEstimate(
            flops=18 * row_total * width * units,
            bytes_accessed=8 * row_total * width + 18 * width * units,
            transcendentals=row_total * units,
        ),
    )(rows, cot_gates, cot_gates, pick, w_gate, w_up, w_down.reshape(units, width))


def body(
    tokens,
    cotangent,
    seq_lengths,
    routes,
    gates,
    norm1_gain,
    w_query,
    key_weight,
    value_weight,
    w_output,
    norm2_gain,
    w_gate,
    w_up,
    w_down,
):
    rows_count, width = tokens.shape
    query_heads = w_query.shape[1] // HEAD_SIZE
    kv_heads = key_weight.shape[1] // HEAD_SIZE
    head_group = query_heads // kv_heads
    local_experts, _, hidden_units = w_gate.shape
    members = lax.axis_size("tensor")
    member_id = lax.axis_index("tensor")
    quarter = rows_count // members
    score_scale = HEAD_SIZE ** (-0.5)
    everyone = ("dp", "tensor")

    def own(rows):
        return lax.dynamic_slice_in_dim(rows, member_id * quarter, quarter, 0)

    def scatter(rows, axes):
        return lax.psum_scatter(
            rows.astype(jnp.bfloat16), axes, scatter_dimension=0, tiled=True
        ).astype(jnp.float32)

    def gather(rows, axes):
        return lax.all_gather(rows.astype(jnp.bfloat16), axes, axis=0, tiled=True)

    expert_ids = jnp.arange(EXPERTS, dtype=jnp.int32)
    gate_dense = jnp.sum(
        jnp.where(own(routes)[:, :, None] == expert_ids, own(gates)[:, :, None], 0.0), axis=1
    )
    gate_high = gate_dense.astype(jnp.bfloat16)
    gate_low = (gate_dense - gate_high.astype(jnp.float32)).astype(jnp.bfloat16)
    blank = jnp.zeros((quarter, LANES - 2 * EXPERTS), jnp.bfloat16)
    own_cot = own(cotangent)
    cot_gates = gather(
        jnp.concatenate([own_cot, gate_high, gate_low, blank], axis=1), everyone
    )
    first_expert = lax.axis_index("dp") * local_experts
    column_expert = first_expert + jnp.arange(local_experts * hidden_units) // hidden_units
    lane = jnp.arange(LANES, dtype=jnp.int32)
    pick = (
        (lane[:, None] % EXPERTS == column_expert[None, :]) & (lane[:, None] < 2 * EXPERTS)
    ).astype(jnp.bfloat16)

    position, allowed = layout(seq_lengths.reshape(-1), rows_count)
    cosine_table, sine_table = rotary(position, HEAD_SIZE)
    inputs = tokens.astype(jnp.float32)
    inv_rms1 = lax.rsqrt(jnp.mean(inputs * inputs, axis=-1, keepdims=True) + EPSILON)
    unit1 = inputs * inv_rms1
    normalized_input = (unit1 * norm1_gain).astype(jnp.bfloat16)
    qkv_weight = jnp.concatenate([w_query, key_weight, value_weight], axis=1)
    query_width = query_heads * HEAD_SIZE
    kv_width = kv_heads * HEAD_SIZE
    qkv = jnp.dot(normalized_input, qkv_weight, preferred_element_type=jnp.float32)
    query_unrotated = qkv[:, :query_width].reshape(rows_count, query_heads, HEAD_SIZE)
    key_unrotated = qkv[:, query_width : query_width + kv_width].reshape(
        rows_count, kv_heads, HEAD_SIZE
    )
    query_matrix = (
        apply_rotation(query_unrotated, cosine_table, sine_table)
        .astype(jnp.bfloat16)
        .reshape(rows_count, kv_heads, head_group, HEAD_SIZE)
    )
    key_rows = apply_rotation(key_unrotated, cosine_table, sine_table).astype(jnp.bfloat16)
    value_matrix = (
        qkv[:, query_width + kv_width :]
        .astype(jnp.bfloat16)
        .reshape(rows_count, kv_heads, HEAD_SIZE)
    )
    raw_scores = (
        jnp.einsum("qkgd,skd->kgqs", query_matrix, key_rows, preferred_element_type=jnp.float32)
        * score_scale
    )
    scores = jnp.where(allowed, raw_scores, -1000000000.0)
    top_score = jnp.max(scores, axis=-1, keepdims=True)
    exponent = jnp.exp(scores - top_score)
    denominator = jnp.sum(exponent, axis=-1, keepdims=True)
    prob_full = exponent / denominator
    prob_low = prob_full.astype(jnp.bfloat16)
    mixed_heads = jnp.einsum(
        "kgqs,skd->qkgd", prob_low, value_matrix, preferred_element_type=jnp.float32
    )
    mixed_heads = mixed_heads.reshape(rows_count, query_width).astype(jnp.bfloat16)
    attended = scatter(
        jnp.dot(mixed_heads, w_output, preferred_element_type=jnp.float32), "tensor"
    )
    hidden = own(inputs) + attended
    inv_rms2 = lax.rsqrt(jnp.mean(hidden * hidden, axis=-1, keepdims=True) + EPSILON)
    unit2 = hidden * inv_rms2
    normed2 = gather(unit2 * norm2_gain, everyone)
    partial_mix, partial_grad, d_gate, d_up, d_down = experts_both_ways(
        normed2, cot_gates, pick, w_gate, w_up, w_down
    )
    grad_norm2 = scatter(partial_grad, everyone)
    mixture = scatter(partial_mix, everyone)
    result = gather(hidden + mixture, "tensor")
    grad_hidden = own_cot.astype(jnp.float32) + norm_back(grad_norm2, unit2, inv_rms2, norm2_gain)
    d_norm2 = jnp.sum(grad_norm2 * unit2, axis=0)
    grad_attended = gather(grad_hidden, "tensor")
    d_output = jnp.einsum(
        "rh,rd->hd", mixed_heads, grad_attended, preferred_element_type=jnp.float32
    )
    d_output = lax.psum(d_output.astype(jnp.bfloat16), "dp").astype(jnp.float32)
    grad_mixed = jnp.einsum(
        "rd,hd->rh", grad_attended, w_output, preferred_element_type=jnp.float32
    )
    grad_mixed = grad_mixed.astype(jnp.bfloat16).reshape(
        rows_count, kv_heads, head_group, HEAD_SIZE
    )
    grad_probs = jnp.einsum(
        "qkgd,skd->kgqs", grad_mixed, value_matrix, preferred_element_type=jnp.float32
    )
    grad_values = jnp.einsum(
        "kgqs,qkgd->skd", prob_low, grad_mixed, preferred_element_type=jnp.float32
    )
    grad_values = grad_values.astype(jnp.bfloat16).reshape(rows_count, kv_width)
    inner_sum = jnp.sum(grad_probs * prob_full, axis=-1, keepdims=True)
    grad_scores = (prob_full * (grad_probs - inner_sum)).astype(jnp.bfloat16)
    grad_queries = (
        jnp.einsum("kgqs,skd->qkgd", grad_scores, key_rows, preferred_element_type=jnp.float32)
        * score_scale
    )
    grad_keys = (
        jnp.einsum("kgqs,qkgd->skd", grad_scores, query_matrix, preferred_element_type=jnp.float32)
        * score_scale
    )
    grad_qpre = apply_rotation(
        grad_queries.reshape(rows_count, query_heads, HEAD_SIZE), cosine_table, -sine_table
    )
    grad_qpre = grad_qpre.astype(jnp.bfloat16).reshape(rows_count, query_width)
    grad_kpre = (
        apply_rotation(grad_keys, cosine_table, -sine_table)
        .astype(jnp.bfloat16)
        .reshape(rows_count, kv_width)
    )
    grad_qkv = jnp.concatenate([grad_qpre, grad_kpre, grad_values], axis=1)
    d_qkv = jnp.einsum("rd,rf->df", normalized_input, grad_qkv, preferred_element_type=jnp.float32)
    d_qkv = lax.psum(d_qkv.astype(jnp.bfloat16), "dp").astype(jnp.float32)
    grad_normed = jnp.einsum("rf,df->rd", grad_qkv, qkv_weight, preferred_element_type=jnp.float32)
    d_norms = lax.psum(jnp.stack([jnp.sum(grad_normed * unit1, axis=0), d_norm2]), everyone)
    grad_norm1 = scatter(grad_normed, "tensor")
    grad_tokens = grad_hidden + norm_back(grad_norm1, own(unit1), own(inv_rms1), norm1_gain)
    return (
        result,
        gather(grad_tokens, "tensor").astype(jnp.float32),
        d_norms[0],
        d_qkv[:, :query_width],
        d_qkv[:, query_width : query_width + kv_width],
        d_qkv[:, query_width + kv_width :],
        d_output,
        d_norms[1],
        d_gate,
        d_up,
        d_down.reshape(w_down.shape),
    )


def solution(mesh):
    in_specs = (
        P("dp", None),
        P("dp", None),
        P("dp", None),
        P("dp", None),
        P("dp", None),
        P(),
        P(None, "tensor"),
        P(None, "tensor"),
        P(None, "tensor"),
        P("tensor", None),
        P(),
        P("dp", None, "tensor"),
        P("dp", None, "tensor"),
        P("dp", "tensor", None),
    )
    out_specs = (
        P("dp", None),
        P("dp", None),
        P(),
        P(None, "tensor"),
        P(None, "tensor"),
        P(None, "tensor"),
        P("tensor", None),
        P(),
        P("dp", None, "tensor"),
        P("dp", None, "tensor"),
        P("dp", "tensor", None),
    )
    return jax.shard_map(body, mesh=mesh, in_specs=in_specs, out_specs=out_specs, check_vma=False)
```

time: 692 us -> 607 us (0.88); the launches traced: 679 us -> 606 us
  local copies, waits for them, and re-layouts: 136 us -> 11.3 us
  waiting for transfers between devices: 360 us -> 464 us
  Pallas kernels: 0 us -> 29.6 us
  other arithmetic: 43.7 us -> 14.1 us
  matrix products: 40 us -> 13.4 us
  starting transfers between devices: 19.6 us -> 0.47 us
  blocking collectives: 64.5 us -> 57.5 us
    reduce_scatter x2 -> x4, waiting for transfers between devices: 136 us -> 282 us  [scatter(): lax.psum_scatter(rows.astype(jnp.bfloat16), axes, scatter_dimension=0, ti...]
    all_gather x2, waiting for transfers between devices: 31.4 us -> 108 us  [gather(): return lax.all_gather(rows.astype(jnp.bfloat16), axes, axis=0, tiled=True)]
    psum x4 -> x1, waiting for transfers between devices: 142 us -> 73.2 us  [body(): d_qkv = lax.psum(d_qkv.astype(jnp.bfloat16), 'dp').astype(jnp.float32)]
    all_to_all x3 -> x0, waiting for transfers between devices: 51.4 us -> none  [the longest x1 32 us: body(): lax.all_to_all(grad_outgoing, 'dp', split_axis=1, concat_axis=1, tiled=True)]
    all_to_all x1 -> x0, blocking collectives: 41.7 us -> none  [body(): lax.all_to_all(outgoing, 'dp', split_axis=1, concat_axis=1, tiled=True)]
    pallas_call x0 -> x1, Pallas kernels: none -> 29.6 us  [experts_both_ways(): pl.pallas_call(expert_kernel, grid=(row_total // tile,), in_specs=[tiled,...]
    dot_general x20 -> x4, matrix products: 35.9 us -> 7.1 us  [the longest x1 2.54 us: body(): jnp.einsum('rf,df->rd', grad_qkv, qkv_weight, preferred_element_type=jnp....]
    gather x4 -> x0, local copies, waits for them, and re-layouts: 26.1 us -> none  [the longest x1 9.6 us: body(): grad_home.reshape(quarter * EXPERTS, width)[lookup]]
  transfers between devices with their start and end apart: 11 -> 7, of which waited for: 8 -> 6; matrix products, arithmetic and copies ran while one was open for 18% -> 2% of each run, Pallas kernels for 0% -> 0%
where the time goes in v1:
time: 607 us; the launch traced here: 606 us
  waiting for transfers between devices  464 us (76%)
  blocking collectives  57.5 us (9%)
  Pallas kernels  29.6 us (5%)
  between operations  15.9 us (3%)
  other arithmetic  14.1 us (2%)
  matrix products  13.4 us (2%)
  local copies, waits for them, and re-layouts  11.3 us (2%)
    reduce_scatter x4, waiting for transfers between devices, scatter(): lax.psum_scatter(rows.astype(jnp.bfloat16), axes, scatter_dimension=0, ti...  282 us
    all_gather x2, waiting for transfers between devices, gather(): return lax.all_gather(rows.astype(jnp.bfloat16), axes, axis=0, tiled=True)  108 us
    psum x1, waiting for transfers between devices, body(): d_qkv = lax.psum(d_qkv.astype(jnp.bfloat16), 'dp').astype(jnp.float32)  73.2 us
    psum x1, blocking collectives, body(): lax.psum(jnp.stack([jnp.sum(grad_normed * unit1, axis=0), d_norm2]), ever...  37.2 us
    pallas_call x1, Pallas kernels, experts_both_ways(): pl.pallas_call(expert_kernel, grid=(row_total // tile,), in_specs=[tiled,...  29.6 us
    all_gather x3, blocking collectives, gather(): return lax.all_gather(rows.astype(jnp.bfloat16), axes, axis=0, tiled=True)  20.3 us
  transfers between devices with their start and end apart: 7, of which 6 were waited for; matrix products, arithmetic and copies ran while one was open for 2% of the time, Pallas kernels for 0%

profile of v1, /device:TPU:0, one launch (start us, length us, event | category | flops | bytes accessed | tf_op | source)
XLA Modules:
  0.0 606.2 jit_solution(2657961872033243285)
XLA Ops:
  9.6 1.2 multiply_reduce_fusion.2
  10.9 1.1 constant_dynamic-update-slice_fusion.2
  12.0 1.0 constant_dynamic-update-slice_fusion.1
  15.0 1.5 fusion.17
  17.5 1.5 fusion.38
  19.7 1.1 convolution_convert_fusion.2
  22.3 23.1 %reduce-scatter.5.cloned.1.call-done = bf16[64,1024]{1,0:T(8,128)(2,1)} async-done(((bf16[256,1024]{1,0:T(8,128)(2,1)}), bf16[64,1024]{1,0:T(8,128)(2,1)}) %reduce-scatter.5.cloned.1.call-update) | async-done | bytes 131088 | tf_op jit(solution)/shard_map/reduce_scatter | solution.py:193
  45.4 1.0 multiply_reduce_fusion.4
  48.1 43.6 %all-gather.5.cloned.1.call-done.cot_ref.gate_ref = bf16[2048,1152]{1,0:T(8,128)(2,1)} async-done(((bf16[64,1152]{1,0:T(8,128)(2,1)}), bf16[2048,1152]{1,0:T(8,128)(2,1)}) %all-gather.5.cloned.1.call-update) | async-done | bytes 4718608 | tf_op jit(solution)/shard_map/all_gather | solution.py:198
  91.8 63.9 %all-gather.3.cloned.1.call-done.rows_ref = bf16[2048,1024]{1,0:T(8,128)(2,1)} async-done(((bf16[64,1024]{1,0:T(8,128)(2,1)}), bf16[2048,1024]{1,0:T(8,128)(2,1)}) %all-gather.3.cloned.1.call-update) | async-done | bytes 4194320 | tf_op jit(solution)/shard_map/all_gather | solution.py:198
  155.7 29.6 %shard_map.221 = (bf16[2048,1024]{1,0:T(8,128)(2,1)}, bf16[2048,1024]{1,0:T(8,128)(2,1)}, f32[4,1024,128]{2,1,0:T(8,128)}, f32[4,1024,128]{2,1,0:T(8,128)}, f32[512,1024]{1,0:T(8,128)}) custom-call(bf16[2048,1024]{1,0:T(8,128)(2,1)} %all-gather.3.cloned.1.call-done.rows_ref, bf16[2048,1152]{1,0:T(8,128)(2,1)} %all-gather.5.cloned.1.call-done.cot_ref.gate_ref, ...), custom_call_target="tpu_custom_call" | custom-call | flops 19327352832 | bytes 26214400 | tf_op jit(solution)/shard_map/pallas_call | solution.py:129
  185.4 139.9 %reduce-scatter.9.cloned.1.call-done = bf16[64,1024]{1,0:T(8,128)(2,1)} async-done(((bf16[2048,1024]{1,0:T(8,128)(2,1)}), bf16[64,1024]{1,0:T(8,128)(2,1)}) %reduce-scatter.9.cloned.1.call-update) | async-done | bytes 131088 | tf_op jit(solution)/shard_map/reduce_scatter | solution.py:193
  325.3 1.1 fusion.13
  326.5 1.0 fusion.35
  327.5 6.5 %all_gather.18 = bf16[256,1024]{1,0:T(8,128)(2,1)S(1)} all-gather(bf16[64,1024]{1,0:T(8,128)(2,1)S(1)} %fusion.35), channel_id=1, replica_groups=mesh['dp'=8,'tensor'=4] {'tensor'}, dimensions={0}, use_global_device_ids=true | all-gather | bytes 655360 | tf_op jit(solution)/shard_map/all_gather | solution.py:198
  334.4 1.0 multiply_reduce_fusion.1
  335.4 1.4 multiply_convert_fusion
  337.3 1.5 fusion.7
  338.9 2.5 multiply_reduce_fusion
  342.5 1.1 convolution_convert_fusion.1
  343.6 1.6 convolution_convert_fusion
  345.2 37.2 %psum.21 = f32[2,1024]{1,0:T(2,128)S(1)} all-reduce(f32[2,1024]{1,0:T(2,128)S(1)} %pad_maximum_fusion.12), channel_id=1, replica_groups=mesh['dp'=8,'tensor'=4] {'dp','tensor'}, use_global_device_ids=true, to_apply=%region_17.18 | all-reduce | flops 2048 | bytes 16384 | tf_op jit(solution)/shard_map/psum | solution.py:313
  383.1 1.0 multiply_reduce_fusion.3
  384.1 119.3 %reduce-scatter.7.cloned.1.call-done = bf16[64,1024]{1,0:T(8,128)(2,1)} async-done(((bf16[2048,1024]{1,0:T(8,128)(2,1)}), bf16[64,1024]{1,0:T(8,128)(2,1)}) %reduce-scatter.7.cloned.1.call-update) | async-done | bytes 131088 | tf_op jit(solution)/shard_map/reduce_scatter | solution.py:193
  503.5 1.2 add_convert_fusion
  504.7 6.5 %all_gather.19 = bf16[256,1024]{1,0:T(8,128)(2,1)S(1)} all-gather(bf16[64,1024]{1,0:T(8,128)(2,1)S(1)} %get-tuple-element.36), channel_id=1, replica_groups=mesh['dp'=8,'tensor'=4] {'tensor'}, dimensions={0}, use_global_device_ids=true | all-gather | bytes 655360 | tf_op jit(solution)/shard_map/all_gather | solution.py:198
  511.2 1.1 convert_element_type.143
  512.3 7.3 %all_gather.17 = bf16[256,1024]{1,0:T(8,128)(2,1)S(1)} all-gather(bf16[64,1024]{1,0:T(8,128)(2,1)S(1)} %get-tuple-element.37), channel_id=1, replica_groups=mesh['dp'=8,'tensor'=4] {'tensor'}, dimensions={0}, use_global_device_ids=true | all-gather | bytes 655360 | tf_op jit(solution)/shard_map/all_gather | solution.py:198
  519.5 73.2 %all-reduce.3.cloned.1.call-done = (bf16[1024,512]{1,0:T(8,128)(2,1)}, bf16[256,1024]{1,0:T(8,128)(2,1)}) async-done(((bf16[1024,512]{1,0:T(8,128)(2,1)}, bf16[256,1024]{1,0:T(8,128)(2,1)}), (bf16[1024,512]{1,0:T(8,128)(2,1)}, bf16[256,1024]{1,0:T(8,128)(2,1)})) %all-reduce.3.cloned.1.call-update) | async-done | bytes 1572880 | tf_op jit(solution)/shard_map/psum | solution.py:311
  592.8 2.1 fusion.36
  594.9 2.1 slice.77
  597.0 1.1 convert_element_type.147
  (92 shorter events, 11.6 us)
Async XLA Ops:
  8.0 11.7 %copy-start = (bf16[256,1024]{1,0:T(8,128)(2,1)S(1)}, bf16[256,1024]{1,0:T(8,128)(2,1)}, u32[]{:S(2)}) copy-start(bf16[256,1024]{1,0:T(8,128)(2,1)} %param.23) | copy-start | bytes 1572868
  8.0 37.4 %reduce-scatter.5.cloned.1.call-start = ((), (), s32[]{:S(2)}) async-start(), calls=%async_computation.4 | async-start | bytes 655360 | tf_op jit(solution)/shard_map/reduce_scatter | solution.py:193
  14.0 1.0 copy-start.2
  17.4 3.5 copy-start.10
  17.4 3.5 copy-start.11
  17.5 3.8 copy-start.6
  19.0 3.3 copy-start.9
  19.0 3.2 copy-start.1
  19.0 27.5 %copy-start.7 = (f32[1024]{0:T(1024)S(1)}, f32[1024]{0:T(1024)}, u32[]{:S(2)}) copy-start(f32[1024]{0:T(1024)} %param.24) | copy-start | bytes 12292
  20.8 70.9 %all-gather.5.cloned.1.call-start = ((), (), s32[]{:S(2)}) async-start(), calls=%async_computation.6 | async-start | bytes 4866048 | tf_op jit(solution)/shard_map/all_gather | solution.py:198
  22.1 133.6 %all-gather.3.cloned.1.call-start = ((), (), s32[]{:S(2)}) async-start(), calls=%async_computation.5 | async-start | bytes 4325376 | tf_op jit(solution)/shard_map/all_gather | solution.py:198
  47.3 278.0 %reduce-scatter.9.cloned.1.call-start = ((), (), s32[]{:S(2)}) async-start(), calls=%async_computation.8 | async-start | bytes 4325376 | tf_op jit(solution)/shard_map/reduce_scatter | solution.py:193
  185.3 149.1 %copy-start.4 = (f32[2,2,256,256]{2,3,1,0:T(8,128)S(1)}, f32[2,2,256,256]{2,3,1,0:T(8,128)}, u32[]{:S(2)}) copy-start(f32[2,2,256,256]{2,3,1,0:T(8,128)} %get-tuple-element.48) | copy-start | bytes 3145732
  185.3 197.7 %reduce-scatter.11.cloned.1.call-start = ((), (), s32[]{:S(2)}) async-start(), calls=%async_computation.9 | async-start | bytes 655360 | tf_op jit(solution)/shard_map/reduce_scatter | solution.py:193
  326.5 1.1 copy-start.12
  338.9 4.6 copy-start.8
  341.5 162.0 %reduce-scatter.7.cloned.1.call-start = ((), (), s32[]{:S(2)}) async-start(), calls=%async_computation.7 | async-start | bytes 4325376 | tf_op jit(solution)/shard_map/reduce_scatter | solution.py:193
  341.5 161.9 %copy-start.3 = (bf16[64,1024]{1,0:T(8,128)(2,1)S(1)}, bf16[64,1024]{1,0:T(8,128)(2,1)}, u32[]{:S(2)}) copy-start(bf16[64,1024]{1,0:T(8,128)(2,1)} %reduce-scatter.9.cloned.1.call-done) | copy-start | bytes 393220
  341.6 161.9 %copy-start.13 = (f32[64]{0:T(128)S(1)}, f32[64]{0:T(128)}, u32[]{:S(2)}) copy-start(f32[64]{0:T(128)} %copy-done.12) | copy-start | bytes 772
  342.2 250.5 %all-reduce.3.cloned.1.call-start = ((), (), s32[]{:S(2)}) async-start(), calls=%async_computation.10 | async-start | bytes 3145728 | tf_op jit(solution)/shard_map/psum | solution.py:311
  592.8 4.2 copy-start.5
Sparse Core Ops, SparseCore 0:
  21.0 24.4 reduce-scatter.4
  341.6 18.7 reduce-scatter.10
  362.7 140.7 reduce-scatter.6
  507.5 85.2 all-reduce.2
Sparse Core Ops, SparseCore 1:
  25.2 66.5 all-gather.4
  95.5 60.1 all-gather.2
  185.4 139.8 reduce-scatter.8

commit v2 on v1

--- a/solution.py
+++ b/solution.py
@@ -1,3 +1,5 @@
+import functools
+
 import jax
 import jax.numpy as jnp
 from jax import lax
@@ -65,6 +67,7 @@
 
 
 def expert_kernel(
+    quarter,
     rows_ref,
     cot_ref,
     gate_ref,
@@ -105,8 +108,15 @@
     grad_gate = (grad_act * up_pre * slope).astype(jnp.bfloat16)
     grad_up = (grad_act * swish).astype(jnp.bfloat16)
     grad_rows = dot(grad_gate, weights[:, :units], 1, 1) + dot(grad_up, weights[:, units:], 1, 1)
-    grad_ref[...] = grad_rows.astype(jnp.bfloat16)
-    mix_ref[...] = dot(activated, w_down_ref[...], 1, 0).astype(jnp.bfloat16)
+    grad_rows = grad_rows.astype(jnp.bfloat16)
+    mix_rows = dot(activated, w_down_ref[...], 1, 0).astype(jnp.bfloat16)
+    members = mix_ref.shape[0]
+    for block in range(rows.shape[0] // (members * quarter)):
+        here = slice(block * quarter, (block + 1) * quarter)
+        for member in range(members):
+            first = (block * members + member) * quarter
+            grad_ref[member, here] = grad_rows[first : first + quarter]
+            mix_ref[member, here] = mix_rows[first : first + quarter]
     total[:, :units] += dot(rows, grad_gate, 0, 0)
     total[:, units:] += dot(rows, grad_up, 0, 0)
     d_down_ref[...] += dot(activated, cot, 0, 0)
@@ -118,16 +128,17 @@
             d_up_ref[e] = total[:, units + e * hidden_units : units + (e + 1) * hidden_units]
 
 
-def experts_both_ways(rows, cot_gates, pick, w_gate, w_up, w_down):
+def experts_both_ways(members, quarter, rows, cot_gates, pick, w_gate, w_up, w_down):
     row_total, width = rows.shape
     experts, _, hidden_units = w_gate.shape
     units = experts * hidden_units
     tile = min(TILE, row_total)
+    sent = pl.BlockSpec((members, tile // members, width), lambda i: (0, i, 0))
     tiled = pl.BlockSpec((tile, width), lambda i: (i, 0))
     flat = pl.BlockSpec((units, width), lambda i: (0, 0))
     deep = pl.BlockSpec((experts, width, hidden_units), lambda i: (0, 0, 0))
     return pl.pallas_call(
-        expert_kernel,
+        functools.partial(expert_kernel, quarter),
         grid=(row_total // tile,),
         in_specs=[
             tiled,
@@ -138,10 +149,10 @@
             deep,
             flat,
         ],
-        out_specs=[tiled, tiled, deep, deep, flat],
+        out_specs=[sent, sent, deep, deep, flat],
         out_shape=[
-            jax.ShapeDtypeStruct((row_total, width), jnp.bfloat16),
-            jax.ShapeDtypeStruct((row_total, width), jnp.bfloat16),
+            jax.ShapeDtypeStruct((members, row_total // members, width), jnp.bfloat16),
+            jax.ShapeDtypeStruct((members, row_total // members, width), jnp.bfloat16),
             jax.ShapeDtypeStruct(w_gate.shape, jnp.float32),
             jax.ShapeDtypeStruct(w_up.shape, jnp.float32),
             jax.ShapeDtypeStruct((units, width), jnp.float32),
@@ -180,6 +191,7 @@
     kv_heads = key_weight.shape[1] // HEAD_SIZE
     head_group = query_heads // kv_heads
     local_experts, _, hidden_units = w_gate.shape
+    sources = lax.axis_size("dp")
     members = lax.axis_size("tensor")
     member_id = lax.axis_index("tensor")
     quarter = rows_count // members
@@ -193,6 +205,15 @@
         return lax.psum_scatter(
             rows.astype(jnp.bfloat16), axes, scatter_dimension=0, tiled=True
         ).astype(jnp.float32)
+
+    def swap(rows):
+        parts = rows.reshape(sources, rows.shape[0] // sources, rows.shape[1])
+        parts = lax.all_to_all(parts, "dp", split_axis=0, concat_axis=0, tiled=True)
+        return jnp.sum(parts.astype(jnp.float32), axis=0)
+
+    def scatter_all(rows):
+        mine = lax.psum_scatter(rows, "tensor", scatter_dimension=0, tiled=True)
+        return swap(mine.reshape(rows.shape[1:]))
 
     def gather(rows, axes):
         return lax.all_gather(rows.astype(jnp.bfloat16), axes, axis=0, tiled=True)
@@ -262,10 +283,10 @@
     unit2 = hidden * inv_rms2
     normed2 = gather(unit2 * norm2_gain, everyone)
     partial_mix, partial_grad, d_gate, d_up, d_down = experts_both_ways(
-        normed2, cot_gates, pick, w_gate, w_up, w_down
-    )
-    grad_norm2 = scatter(partial_grad, everyone)
-    mixture = scatter(partial_mix, everyone)
+        members, quarter, normed2, cot_gates, pick, w_gate, w_up, w_down
+    )
+    grad_norm2 = scatter_all(partial_grad)
+    mixture = scatter_all(partial_mix)
     result = gather(hidden + mixture, "tensor")
     grad_hidden = own_cot.astype(jnp.float32) + norm_back(grad_norm2, unit2, inv_rms2, norm2_gain)
     d_norm2 = jnp.sum(grad_norm2 * unit2, axis=0)
@@ -273,7 +294,6 @@
     d_output = jnp.einsum(
         "rh,rd->hd", mixed_heads, grad_attended, preferred_element_type=jnp.float32
     )
-    d_output = lax.psum(d_output.astype(jnp.bfloat16), "dp").astype(jnp.float32)
     grad_mixed = jnp.einsum(
         "rd,hd->rh", grad_attended, w_output, preferred_element_type=jnp.float32
     )
@@ -308,9 +328,15 @@
     )
     grad_qkv = jnp.concatenate([grad_qpre, grad_kpre, grad_values], axis=1)
     d_qkv = jnp.einsum("rd,rf->df", normalized_input, grad_qkv, preferred_element_type=jnp.float32)
-    d_qkv = lax.psum(d_qkv.astype(jnp.bfloat16), "dp").astype(jnp.float32)
+    d_both = jnp.concatenate(
+        [d_qkv.astype(jnp.bfloat16), d_output.astype(jnp.bfloat16).reshape(-1, d_qkv.shape[1])]
+    )
+    d_both = gather(swap(d_both), "dp").astype(jnp.float32)
+    d_qkv = d_both[:width]
+    d_output = d_both[width:].reshape(w_output.shape)
     grad_normed = jnp.einsum("rf,df->rd", grad_qkv, qkv_weight, preferred_element_type=jnp.float32)
-    d_norms = lax.psum(jnp.stack([jnp.sum(grad_normed * unit1, axis=0), d_norm2]), everyone)
+    d_norms = jnp.stack([jnp.sum(grad_normed * unit1, axis=0), d_norm2])
+    d_norms = jnp.sum(lax.all_gather(d_norms, everyone, axis=0), axis=0)
     grad_norm1 = scatter(grad_normed, "tensor")
     grad_tokens = grad_hidden + norm_back(grad_norm1, own(unit1), own(inv_rms1), norm1_gain)
     return (

time: 607 us -> 415 us (0.68)
  waiting for transfers between devices: 464 us -> 209 us
  blocking collectives: 57.5 us -> 113 us
  starting transfers between devices: 0.47 us -> 7.52 us
    reduce_scatter x4 -> x2, waiting for transfers between devices: 282 us -> 23.2 us  [scatter(): lax.psum_scatter(rows.astype(jnp.bfloat16), axes, scatter_dimension=0, ti...]
    psum x1 -> x0, waiting for transfers between devices: 73.2 us -> none  [body(): d_qkv = lax.psum(d_qkv.astype(jnp.bfloat16), 'dp').astype(jnp.float32)]
    all_gather x0 -> x1, blocking collectives: none -> 55 us  [body(): d_norms = jnp.sum(lax.all_gather(d_norms, everyone, axis=0), axis=0)]
    reduce_scatter x0 -> x2, waiting for transfers between devices: none -> 42.7 us  [scatter_all(): mine = lax.psum_scatter(rows, 'tensor', scatter_dimension=0, tiled=True)]
    psum x1 -> x0, blocking collectives: 37.2 us -> none  [body(): lax.psum(jnp.stack([jnp.sum(grad_normed * unit1, axis=0), d_norm2]), ever...]
    all_to_all x0 -> x2, waiting for transfers between devices: none -> 34.6 us  [swap(): parts = lax.all_to_all(parts, 'dp', split_axis=0, concat_axis=0, tiled=True)]
    all_to_all x0 -> x1, blocking collectives: none -> 31.3 us  [swap(): parts = lax.all_to_all(parts, 'dp', split_axis=0, concat_axis=0, tiled=True)]
    all_to_all x0 -> x2, starting transfers between devices: none -> 7.23 us  [swap(): parts = lax.all_to_all(parts, 'dp', split_axis=0, concat_axis=0, tiled=True)]
  transfers between devices with their start and end apart: 7 -> 9, of which waited for: 6 -> 5; matrix products, arithmetic and copies ran while one was open for 2% -> 5% of each run, Pallas kernels for 0% -> 0%
where the time goes in v2:
time: 415 us; the launch traced here: 414 us
  waiting for transfers between devices  209 us (50%)
  blocking collectives  113 us (27%)
  Pallas kernels  29.6 us (7%)
  between operations  16.1 us (4%)
  local copies, waits for them, and re-layouts  13.3 us (3%)
  matrix products  13 us (3%)
  other arithmetic  12.6 us (3%)
  starting transfers between devices  7.52 us (2%)
    all_gather x3, waiting for transfers between devices, gather(): return lax.all_gather(rows.astype(jnp.bfloat16), axes, axis=0, tiled=True)  108 us
    all_gather x1, blocking collectives, body(): d_norms = jnp.sum(lax.all_gather(d_norms, everyone, axis=0), axis=0)  55 us
    reduce_scatter x2, waiting for transfers between devices, scatter_all(): mine = lax.psum_scatter(rows, 'tensor', scatter_dimension=0, tiled=True)  42.7 us
    all_to_all x2, waiting for transfers between devices, swap(): parts = lax.all_to_all(parts, 'dp', split_axis=0, concat_axis=0, tiled=True)  34.6 us
    all_to_all x1, blocking collectives, swap(): parts = lax.all_to_all(parts, 'dp', split_axis=0, concat_axis=0, tiled=True)  31.3 us
    pallas_call x1, Pallas kernels, experts_both_ways(): pl.pallas_call(functools.partial(expert_kernel, quarter), grid=(row_total...  29.6 us
    all_gather x3, blocking collectives, gather(): return lax.all_gather(rows.astype(jnp.bfloat16), axes, axis=0, tiled=True)  26.5 us
    reduce_scatter x2, waiting for transfers between devices, scatter(): lax.psum_scatter(rows.astype(jnp.bfloat16), axes, scatter_dimension=0, ti...  23.2 us
  transfers between devices with their start and end apart: 9, of which 5 were waited for; matrix products, arithmetic and copies ran while one was open for 5% of the time, Pallas kernels for 0%

profile of v2, /device:TPU:0, one launch (start us, length us, event | category | flops | bytes accessed | tf_op | source)
XLA Modules:
  0.0 413.6 jit_solution(18419378592443377472)
XLA Ops:
  9.7 1.2 multiply_reduce_fusion.2
  11.0 1.9 constant_dynamic-update-slice_fusion.2
  12.8 1.7 constant_dynamic-update-slice_fusion.1
  15.2 1.7 fusion.11
  17.9 1.5 fusion.32
  20.2 1.1 convolution_convert_fusion.2
  22.8 23.1 %reduce-scatter.5.cloned.1.call-done = bf16[64,1024]{1,0:T(8,128)(2,1)} async-done(((bf16[256,1024]{1,0:T(8,128)(2,1)}), bf16[64,1024]{1,0:T(8,128)(2,1)}) %reduce-scatter.5.cloned.1.call-update) | async-done | bytes 131088 | tf_op jit(solution)/shard_map/reduce_scatter | solution.py:205
  46.0 1.0 multiply_reduce_fusion.6
  48.7 43.6 %all-gather.8.cloned.1.call-done.cot_ref.gate_ref = bf16[2048,1152]{1,0:T(8,128)(2,1)} async-done(((bf16[64,1152]{1,0:T(8,128)(2,1)}), bf16[2048,1152]{1,0:T(8,128)(2,1)}) %all-gather.8.cloned.1.call-update) | async-done | bytes 4718608 | tf_op jit(solution)/shard_map/all_gather | solution.py:219
  92.3 63.9 %all-gather.6.cloned.1.call-done.rows_ref = bf16[2048,1024]{1,0:T(8,128)(2,1)} async-done(((bf16[64,1024]{1,0:T(8,128)(2,1)}), bf16[2048,1024]{1,0:T(8,128)(2,1)}) %all-gather.6.cloned.1.call-update) | async-done | bytes 4194320 | tf_op jit(solution)/shard_map/all_gather | solution.py:219
  156.2 29.6 %shard_map.221 = (bf16[4,512,1024]{2,1,0:T(8,128)(2,1)}, bf16[4,512,1024]{2,1,0:T(8,128)(2,1)}, f32[4,1024,128]{2,1,0:T(8,128)}, f32[4,1024,128]{2,1,0:T(8,128)}, f32[512,1024]{1,0:T(8,128)}) custom-call(bf16[2048,1024]{1,0:T(8,128)(2,1)} %all-gather.6.cloned.1.call-done.rows_ref, bf16[2048,1152]{1,0:T(8,128)(2,1)} %all-gather.8.cloned.1.call-done.cot_ref.gate_ref, ...), custom_call_target="tpu_custom_call" | custom-call | flops 19327352832 | bytes 26214400 | tf_op jit(solution)/shard_map/pallas_call | solution.py:140
  186.6 42.7 %reduce-scatter.9.cloned.1.call-done = bf16[1,512,1024]{2,1,0:T(8,128)(2,1)} async-done(((bf16[4,512,1024]{2,1,0:T(8,128)(2,1)}), bf16[1,512,1024]{2,1,0:T(8,128)(2,1)}) %reduce-scatter.9.cloned.1.call-update) | async-done | bytes 1048592 | tf_op jit(solution)/shard_map/reduce_scatter | solution.py:215
  229.3 31.3 %all_to_all.15 = bf16[8,64,1024]{2,1,0:T(8,128)(2,1)S(1)} all-to-all(bf16[8,64,1024]{2,1,0:T(8,128)(2,1)} %bitcast.109), channel_id=1, replica_groups=mesh['dp'=8,'tensor'=4] {'dp'}, dimensions={0} | all-to-all | bytes 2097152 | tf_op jit(solution)/shard_map/all_to_all | solution.py:211
  261.6 10.4 %all_gather.27 = bf16[256,1024]{1,0:T(8,128)(2,1)S(1)} all-gather(bf16[64,1024]{1,0:T(8,128)(2,1)S(1)} %fusion.29), channel_id=1, replica_groups=mesh['dp'=8,'tensor'=4] {'tensor'}, dimensions={0}, use_global_device_ids=true | all-gather | bytes 655360 | tf_op jit(solution)/shard_map/all_gather | solution.py:219
  272.9 1.7 multiply_reduce_fusion.1
  276.1 1.6 fusion.7
  278.3 1.3 pad_maximum_fusion
  279.6 3.6 all-to-all-start.2
  283.2 2.9 multiply_reduce_fusion
  286.2 34.6 %all-to-all-done.2 = bf16[8,192,512]{2,1,0:T(8,128)(2,1)S(1)} async-done(((bf16[8,192,512]{2,1,0:T(8,128)(2,1)}), bf16[8,192,512]{2,1,0:T(8,128)(2,1)S(1)}, u32[]{:S(2)}, u32[]{:S(2)}) %all-to-all-start.2) | async-done | bytes 1572896 | tf_op jit(solution)/shard_map/all_to_all | solution.py:211
  320.8 3.6 all-to-all-start
  324.5 0.9 reduce_sum.165
  325.6 55.0 %all-gather.1 = f32[32,2,1024]{2,1,0:T(2,128)S(1)} all-gather(f32[1,2,1024]{2,1,0:T(2,128)S(1)} %maximum_bitcast_fusion.5), channel_id=2, replica_groups=mesh['dp'=8,'tensor'=4] {'dp','tensor'}, dimensions={0}, use_global_device_ids=true | all-gather | bytes 270336 | tf_op jit(solution)/shard_map/all_gather | solution.py:339
  381.4 1.0 multiply_reduce_fusion.4
  382.5 1.2 add_convert_fusion
  383.7 8.3 %all_gather.28 = bf16[256,1024]{1,0:T(8,128)(2,1)S(1)} all-gather(bf16[64,1024]{1,0:T(8,128)(2,1)S(1)} %get-tuple-element.34), channel_id=1, replica_groups=mesh['dp'=8,'tensor'=4] {'tensor'}, dimensions={0}, use_global_device_ids=true | all-gather | bytes 655360 | tf_op jit(solution)/shard_map/all_gather | solution.py:219
  392.0 1.1 convert_element_type.142
  393.1 7.7 %all_gather.26 = bf16[256,1024]{1,0:T(8,128)(2,1)} all-gather(bf16[64,1024]{1,0:T(8,128)(2,1)S(1)} %get-tuple-element.35), channel_id=1, replica_groups=mesh['dp'=8,'tensor'=4] {'tensor'}, dimensions={0}, use_global_device_ids=true | all-gather | bytes 655360 | tf_op jit(solution)/shard_map/all_gather | solution.py:219
  400.8 1.3 slice.88
  402.1 1.3 reshape.244
  403.4 1.0 fusion.30
  404.4 1.0 slice.85
  (138 shorter events, 13.4 us)
Async XLA Ops:
  8.0 12.2 %copy-start = (bf16[256,1024]{1,0:T(8,128)(2,1)S(1)}, bf16[256,1024]{1,0:T(8,128)(2,1)}, u32[]{:S(2)}) copy-start(bf16[256,1024]{1,0:T(8,128)(2,1)} %param.23) | copy-start | bytes 1572868
  8.0 7.2 %copy-start.2 = (bf16[256,1024]{1,0:T(8,128)(2,1)S(1)}, bf16[256,1024]{1,0:T(8,128)(2,1)}, u32[]{:S(2)}) copy-start(bf16[256,1024]{1,0:T(8,128)(2,1)} %param.14) | copy-start | bytes 1572868
  8.0 6.5 %copy-start.11 = (bf16[1024,128]{1,0:T(8,128)(2,1)S(1)}, bf16[1024,128]{1,0:T(8,128)(2,1)}, u32[]{:S(2)}) copy-start(bf16[1024,128]{1,0:T(8,128)(2,1)} %param.22) | copy-start | bytes 786436
  8.0 7.2 %copy-start.20 = (f32[1024]{0:T(1024)S(1)}, f32[1024]{0:T(1024)}, u32[]{:S(2)}) copy-start(f32[1024]{0:T(1024)} %param.19) | copy-start | bytes 12292
  8.1 37.9 %reduce-scatter.5.cloned.1.call-start = ((), (), s32[]{:S(2)}) async-start(), calls=%async_computation.7 | async-start | bytes 655360 | tf_op jit(solution)/shard_map/reduce_scatter | solution.py:205
  11.0 6.0 %copy-start.21 = (f32[256]{0:T(256)}, f32[256]{0:T(256)S(1)}, u32[]{:S(2)}) copy-start(f32[256]{0:T(256)S(1)} %add_rsqrt_fusion) | copy-start | bytes 3076
  17.2 3.0 copy-start.17
  17.7 2.4 copy-start.9
  17.8 2.4 copy-start.12
  17.8 2.4 copy-start.14
  17.9 2.3 copy-start.18
  19.4 2.0 copy-start.27
  19.4 2.1 copy-start.28
  19.4 2.4 copy-start.8
  21.3 25.7 %copy-start.16 = (f32[1024]{0:T(1024)S(1)}, f32[1024]{0:T(1024)}, u32[]{:S(2)}) copy-start(f32[1024]{0:T(1024)} %param.24) | copy-start | bytes 12292
  21.4 70.9 %all-gather.8.cloned.1.call-start = ((), (), s32[]{:S(2)}) async-start(), calls=%async_computation.9 | async-start | bytes 4866048 | tf_op jit(solution)/shard_map/all_gather | solution.py:219
  22.7 133.5 %all-gather.6.cloned.1.call-start = ((), (), s32[]{:S(2)}) async-start(), calls=%async_computation.8 | async-start | bytes 4325376 | tf_op jit(solution)/shard_map/all_gather | solution.py:219
  47.8 181.5 %reduce-scatter.9.cloned.1.call-start = ((), (), s32[]{:S(2)}) async-start(), calls=%async_computation.11 | async-start | bytes 5242880 | tf_op jit(solution)/shard_map/reduce_scatter | solution.py:215
  185.8 100.4 %reduce-scatter.7.cloned.1.call-start = ((), (), s32[]{:S(2)}) async-start(), calls=%async_computation.10 | async-start | bytes 5242880 | tf_op jit(solution)/shard_map/reduce_scatter | solution.py:215
  261.4 10.6 %copy-start.29 = (f32[64]{0:T(128)}, f32[64]{0:T(128)S(1)}, u32[]{:S(2)}) copy-start(f32[64]{0:T(128)S(1)} %broadcast_multiply_fusion.2) | copy-start | bytes 772
  261.6 11.3 %copy-start.19 = (bf16[256,128]{0,1:T(8,128)(2,1)S(1)}, bf16[256,128]{0,1:T(8,128)(2,1)}, u32[]{:S(2)}) copy-start(bf16[256,128]{0,1:T(8,128)(2,1)} %copy-done.18) | copy-start | bytes 196612
  261.6 11.3 %copy-start.25 = (f32[2,2,256]{2,1,0:T(2,128)S(1)}, f32[2,2,256]{2,1,0:T(2,128)}, u32[]{:S(2)}) copy-start(f32[2,2,256]{2,1,0:T(2,128)} %copy-done.24) | copy-start | bytes 12292
  279.6 41.3 %all-to-all-start.2 = ((bf16[8,192,512]{2,1,0:T(8,128)(2,1)}), bf16[8,192,512]{2,1,0:T(8,128)(2,1)S(1)}, u32[]{:S(2)}, u32[]{:S(2)}) async-start(bf16[8,192,512]{2,1,0:T(8,128)(2,1)} %bitcast.105), calls=%async_computation.6 | async-start | bytes 3145728 | tf_op jit(solution)/shard_map/all_to_all | solution.py:211
  283.2 98.2 %reduce-scatter.11.cloned.1.call-start = ((), (), s32[]{:S(2)}) async-start(), calls=%async_computation.12 | async-start | bytes 655360 | tf_op jit(solution)/shard_map/reduce_scatter | solution.py:205
  286.2 39.3 %copy-start.23 = (f32[256]{0:T(256)S(1)}, f32[256]{0:T(256)}, u32[]{:S(2)}) copy-start(f32[256]{0:T(256)} %copy-done.21) | copy-start | bytes 3076
  320.8 59.8 %all-to-all-start = ((bf16[8,64,1024]{2,1,0:T(8,128)(2,1)}), bf16[8,64,1024]{2,1,0:T(8,128)(2,1)S(1)}, u32[]{:S(2)}, u32[]{:S(2)}) async-start(bf16[8,64,1024]{2,1,0:T(8,128)(2,1)} %bitcast.108), calls=%async_computation.2 | async-start | bytes 2097152 | tf_op jit(solution)/shard_map/all_to_all | solution.py:211
  324.5 58.0 %copy-start.30 = (f32[64]{0:T(128)S(1)}, f32[64]{0:T(128)}, u32[]{:S(2)}) copy-start(f32[64]{0:T(128)} %copy-done.29) | copy-start | bytes 772
  324.5 76.3 %all-gather.10.cloned.1.call-start = ((), (), s32[]{:S(2)}) async-start(), calls=%async_computation.13 | async-start | bytes 1769472 | tf_op jit(solution)/shard_map/all_gather | solution.py:219
  325.4 56.0 %copy-start.5 = (f32[256,1024]{1,0:T(8,128)S(1)}, f32[256,1024]{1,0:T(8,128)}, u32[]{:S(2)}) copy-start(f32[256,1024]{1,0:T(8,128)} %get-tuple-element.29) | copy-start | bytes 3145732
  325.4 57.1 %copy-start.4 = (f32[64,1024]{1,0:T(8,128)S(1)}, f32[64,1024]{1,0:T(8,128)}, u32[]{:S(2)}) copy-start(f32[64,1024]{1,0:T(8,128)} %copy-done.3) | copy-start | bytes 786436
  400.8 2.6 copy-start.1
  403.4 2.1 copy-start.6
  (8 other events, 9.5 us)
Sparse Core Ops, SparseCore 0:
  21.5 24.4 reduce-scatter.4
  185.9 43.2 reduce-scatter.8
  231.8 47.3 reduce-scatter.6
  286.9 22.3 reduce-scatter.10
Sparse Core Ops, SparseCore 1:
  25.8 66.4 all-gather.7
  96.0 60.1 all-gather.5
  327.7 51.8 all-gather.9
